TPU v7x, 512 devices: a whole 4x8x8 slice. The times are simulated.
512 devices in a mesh: layer: 16 (over y, core), grid: 32 (over x, z).
Axes of the slice: x: 4, y: 8, z: 8, core: 2. Of those that a mesh axis runs over, the one named last changes fastest.
Arguments:
- l_panels: bfloat16 [16, 2, 8192, 512], P('layer', None, 'grid'), may hold values from -6 to 6
- u_panels: bfloat16 [16, 2, 512, 2048], P('layer', None, 'grid'), may hold values from -0.046875 to 0.046875
- panel_fill: int32 [16, 2, 64, 4], P('layer', None, 'grid'), may hold values 0 or 1
- copy_fill: int32 [16, 64, 16], P('layer', 'grid'), may hold values 0 or 1
- sep_panels: bfloat16 [15, 8192, 256], P(None, 'grid'), may hold values from -0.25 to 0.25
- sep_owner: int32 [15], replicated, may hold values from 0 to 31
Outputs:
- schur: float32 [8192, 2048], P('grid', 'layer')
All inputs are finite; a program needn't handle non-finite values. No bound on the sum of `panel_fill` or of `copy_fill` on one device may be relied on, other than what follows from the above.
Results may differ from a plain program's by a relative error of at most 0.0035.
Values may be sent and summed in bfloat16 or wider, within the bound.
A program may use at most 64 MiB of HBM per device.

v0:
```python
import jax
import jax.numpy as jnp
from jax import lax
from jax.sharding import PartitionSpec as P

BLOCK = 128


def from_partner(x, axis, apart):
    return lax.ppermute(x, axis, [(i, i ^ 1 << apart) for i in range(lax.axis_size(axis))])


def spread(x, axis, root):
    mine = lax.axis_index(axis) == root
    return lax.psum(jnp.where(mine, x, jnp.zeros_like(x)), axis)


def local(l_panels, u_panels, panel_fill, copy_fill, sep_panels, sep_owner):
    panel_count = l_panels.shape[1]
    row_count = l_panels.shape[2]
    panel_width = l_panels.shape[3]
    columns = u_panels.shape[3]
    fill_panel = panel_fill[0].astype(jnp.bfloat16)
    masked = (
        l_panels[0].reshape(panel_count, row_count // BLOCK, BLOCK, panel_width // BLOCK, BLOCK)
        * fill_panel[:, :, None, :, None]
    ).reshape(panel_count, row_count, panel_width)
    running = jnp.zeros((row_count, columns), jnp.float32)
    piece = lax.all_gather(u_panels, "grid", axis=2, tiled=True)
    for k in range(panel_count):
        column_part = masked[k]
        running = running + jnp.dot(column_part, piece[0, k], preferred_element_type=jnp.float32)
    fill_copy = copy_fill[0].astype(jnp.float32)
    layer_copy = -(
        running.reshape(row_count // BLOCK, BLOCK, columns // BLOCK, BLOCK)
        * fill_copy[:, None, :, None]
    ).reshape(row_count, columns)
    layers = lax.axis_size("layer")
    level_count = layers.bit_length() - 1
    layer_index = lax.axis_index("layer")
    column_width = columns // layers
    combined = layer_copy
    for level_index in range(level_count):
        partner = from_partner(combined, "layer", level_index)
        combined = combined + partner
        node_index = layers - (layers >> level_index) + (layer_index >> level_index + 1)
        owner_index = sep_owner[node_index]
        pivot_rows = spread(combined.astype(jnp.bfloat16), "grid", owner_index)
        factor = lax.dynamic_index_in_dim(sep_panels, node_index, 0, keepdims=False)
        combined = combined - jnp.dot(factor, pivot_rows, preferred_element_type=jnp.float32)
    return lax.dynamic_slice_in_dim(combined, layer_index * column_width, column_width, 1)


def solution(mesh):
    return jax.shard_map(
        local,
        mesh=mesh,
        in_specs=(
            P("layer", None, "grid", None),
            P("layer", None, "grid", None),
            P("layer", None, "grid", None),
            P("layer", "grid", None),
            P(None, "grid", None),
            P(),
        ),
        out_specs=P("grid", "layer"),
        check_vma=False,
    )
```

profile of v0, /device:TPU:8, one launch (start us, length us, event | category | flops | bytes accessed | tf_op | source)
XLA Modules:
  0.0 1016.5 jit_solution(16947582631460522231)
XLA Ops:
  6.5 0.0 copy-start
  6.5 0.0 all-gather.2.cloned.1.call-start
  6.5 0.7 all-gather.2.cloned.1.call-update
  7.3 0.0 all-reduce.5.cloned.1.call-start
  7.3 1.2 reshape_squeeze.3
  8.5 0.7 convert_bitcast_fusion
  9.2 0.7 convert_bitcast_fusion.1
  9.8 0.3 broadcast_multiply_fusion
  10.2 0.2 fusion.20
  10.3 93.3 %all-gather.2.cloned.1.call-done = bf16[1,2,512,2048]{3,2,1,0:T(8,128)(2,1)} async-done(((bf16[1,2,16,2048]{3,2,1,0:T(8,128)(2,1)}), bf16[1,2,512,2048]{3,2,1,0:T(8,128)(2,1)}) %all-gather.2.cloned.1.call-update) | async-done | bytes 4194320 | tf_op jit(solution)/shard_map/all_gather | solution.py:29
  103.6 0.0 copy-start.1
  103.6 2.4 fusion.2
  106.1 0.2 mul.24
  106.3 0.2 copy-done.1
  106.4 0.0 copy-start.2
  106.4 2.5 fusion.1
  109.0 1.9 collective-permute-start
  110.9 0.0 copy-done.2
  110.9 0.7 fusion.21
  112.2 3.1 collective-permute-done
  115.4 4.4 convert_select_fusion.3
  119.8 0.0 all-reduce.5.cloned.1.call-update
  119.8 0.0 all-reduce.7.cloned.1.call-start
  119.9 157.3 %all-reduce.5.cloned.1.call-done = bf16[256,2048]{1,0:T(8,128)(2,1)} async-done(((bf16[256,2048]{1,0:T(8,128)(2,1)}), bf16[256,2048]{1,0:T(8,128)(2,1)}) %all-reduce.5.cloned.1.call-update) | async-done | bytes 1048592 | tf_op jit(solution)/shard_map/psum | solution.py:15
  277.2 0.0 copy-done
  277.2 3.7 convolution_subtract_fusion.2
  280.9 2.4 collective-permute-start.1
  283.9 41.9 %collective-permute-done.1 = f32[256,2048]{1,0:T(8,128)} collective-permute-done((f32[256,2048]{1,0:T(8,128)}, f32[256,2048]{1,0:T(8,128)}, u32[]{:S(2)}, u32[]{:S(2)}) %collective-permute-start.1) | collective-permute-done | bytes 2097184 | tf_op jit(solution)/shard_map/ppermute | solution.py:10
  325.9 4.4 convert_select_fusion.2
  330.3 0.0 all-reduce.7.cloned.1.call-update
  330.3 0.0 all-reduce.9.cloned.1.call-start
  330.4 158.1 %all-reduce.7.cloned.1.call-done = bf16[256,2048]{1,0:T(8,128)(2,1)} async-done(((bf16[256,2048]{1,0:T(8,128)(2,1)}), bf16[256,2048]{1,0:T(8,128)(2,1)}) %all-reduce.7.cloned.1.call-update) | async-done | bytes 1048592 | tf_op jit(solution)/shard_map/psum | solution.py:15
  488.5 3.7 convolution_subtract_fusion.1
  492.2 4.3 collective-permute-start.2
  497.1 85.0 %collective-permute-done.2 = f32[256,2048]{1,0:T(8,128)} collective-permute-done((f32[256,2048]{1,0:T(8,128)}, f32[256,2048]{1,0:T(8,128)}, u32[]{:S(2)}, u32[]{:S(2)}) %collective-permute-start.2) | collective-permute-done | bytes 2097184 | tf_op jit(solution)/shard_map/ppermute | solution.py:10
  582.0 4.4 convert_select_fusion.1
  586.5 0.0 all-reduce.9.cloned.1.call-update
  586.5 0.0 all-reduce.11.cloned.1.call-start
  586.5 159.1 %all-reduce.9.cloned.1.call-done = bf16[256,2048]{1,0:T(8,128)(2,1)} async-done(((bf16[256,2048]{1,0:T(8,128)(2,1)}), bf16[256,2048]{1,0:T(8,128)(2,1)}) %all-reduce.9.cloned.1.call-update) | async-done | bytes 1048592 | tf_op jit(solution)/shard_map/psum | solution.py:15
  745.7 3.7 convolution_subtract_fusion
  749.4 6.5 collective-permute-start.3
  756.4 87.0 %collective-permute-done.3 = f32[256,2048]{1,0:T(8,128)} collective-permute-done((f32[256,2048]{1,0:T(8,128)}, f32[256,2048]{1,0:T(8,128)}, u32[]{:S(2)}, u32[]{:S(2)}) %collective-permute-start.3) | collective-permute-done | bytes 2097184 | tf_op jit(solution)/shard_map/ppermute | solution.py:10
  843.5 4.4 convert_select_fusion
  847.9 0.0 all-reduce.11.cloned.1.call-update
  847.9 158.8 %all-reduce.11.cloned.1.call-done = bf16[256,2048]{1,0:T(8,128)(2,1)} async-done(((bf16[256,2048]{1,0:T(8,128)(2,1)}), bf16[256,2048]{1,0:T(8,128)(2,1)}) %all-reduce.11.cloned.1.call-update) | async-done | bytes 1048592 | tf_op jit(solution)/shard_map/psum | solution.py:15
  1006.7 1.7 fusion.7
  1008.4 1.6 dynamic-slice_subtract_fusion
Async XLA Ops:
  6.5 270.6 %copy-start = (bf16[15,256,256]{2,1,0:T(8,128)(2,1)S(1)}, bf16[15,256,256]{2,1,0:T(8,128)(2,1)}, u32[]{:S(2)}) copy-start(bf16[15,256,256]{2,1,0:T(8,128)(2,1)} %param.10) | copy-start | bytes 5898244
  6.5 97.1 %all-gather.2.cloned.1.call-start = ((), (), s32[]{:S(2)}) async-start(), calls=%async_computation | async-start | bytes 4325376 | tf_op jit(solution)/shard_map/all_gather | solution.py:29
  7.3 269.9 %all-reduce.5.cloned.1.call-start = ((), (), s32[]{:S(2)}) async-start(), calls=%async_computation.1 | async-start | bytes 2097152 | tf_op jit(solution)/shard_map/psum | solution.py:15
  103.6 2.8 copy-start.1
  106.4 4.5 copy-start.2
  109.0 6.4 collective-permute-start
  119.8 368.7 %all-reduce.7.cloned.1.call-start = ((), (), s32[]{:S(2)}) async-start(), calls=%async_computation.2 | async-start | bytes 2097152 | tf_op jit(solution)/shard_map/psum | solution.py:15
  280.9 45.0 %collective-permute-start.1 = (f32[256,2048]{1,0:T(8,128)}, f32[256,2048]{1,0:T(8,128)}, u32[]{:S(2)}, u32[]{:S(2)}) collective-permute-start(f32[256,2048]{1,0:T(8,128)} %convolution_subtract_fusion.2), channel_id=1, source_target_pairs={{0,64},{32,96},{64,0},{96,32},{128,192},{160,224},{192,128},{224,1... | collective-permute-start | bytes 6291464 | tf_op jit(solution)/shard_map/ppermute | solution.py:10
  330.3 415.3 %all-reduce.9.cloned.1.call-start = ((), (), s32[]{:S(2)}) async-start(), calls=%async_computation.3 | async-start | bytes 2097152 | tf_op jit(solution)/shard_map/psum | solution.py:15
  492.2 89.9 %collective-permute-start.2 = (f32[256,2048]{1,0:T(8,128)}, f32[256,2048]{1,0:T(8,128)}, u32[]{:S(2)}, u32[]{:S(2)}) collective-permute-start(f32[256,2048]{1,0:T(8,128)} %convolution_subtract_fusion.1), channel_id=1, source_target_pairs={{0,128},{32,160},{64,192},{96,224},{128,0},{160,32},{192,64},{224,... | collective-permute-start | bytes 6291464 | tf_op jit(solution)/shard_map/ppermute | solution.py:10
  586.5 420.2 %all-reduce.11.cloned.1.call-start = ((), (), s32[]{:S(2)}) async-start(), calls=%async_computation.4 | async-start | bytes 2097152 | tf_op jit(solution)/shard_map/psum | solution.py:15
  749.4 94.1 %collective-permute-start.3 = (f32[256,2048]{1,0:T(8,128)}, f32[256,2048]{1,0:T(8,128)}, u32[]{:S(2)}, u32[]{:S(2)}) collective-permute-start(f32[256,2048]{1,0:T(8,128)} %convolution_subtract_fusion), channel_id=1, source_target_pairs={{0,256},{32,288},{64,320},{96,352},{128,384},{160,416},{192,448},{... | collective-permute-start | bytes 6291464 | tf_op jit(solution)/shard_map/ppermute | solution.py:10
Sparse Core Ops, SparseCore 0:
  10.5 93.0 all-gather.1
  119.9 157.1 all-reduce.4
  330.5 157.9 all-reduce.6
  586.6 159.0 all-reduce.8
  848.0 158.6 all-reduce.10
where the time goes:
time: 1020 us
  waiting for transfers between devices  944 us (93%)
  other arithmetic  21 us (2%)
  matrix products  17.7 us (2%)
  between operations  15.7 us (2%)
  starting transfers between devices  15.3 us (2%)
    psum x4, waiting for transfers between devices, spread(): return lax.psum(jnp.where(mine, x, jnp.zeros_like(x)), axis)  633 us
    ppermute x4, waiting for transfers between devices, from_partner(): lax.ppermute(x, axis, [(i, i ^ 1 << apart) for i in range(lax.axis_size(a...  217 us
    all_gather x1, waiting for transfers between devices, local(): piece = lax.all_gather(u_panels, 'grid', axis=2, tiled=True)  93.3 us
  transfers between devices with their start and end apart: 9, of which 9 were waited for; matrix products, arithmetic and copies ran while one was open for 0% of the time, Pallas kernels for 0%

commit v1 on v0

--- a/solution.py
+++ b/solution.py
@@ -12,7 +12,7 @@
 
 def spread(x, axis, root):
     mine = lax.axis_index(axis) == root
-    return lax.psum(jnp.where(mine, x, jnp.zeros_like(x)), axis)
+    return jnp.sum(lax.all_gather(jnp.where(mine, x, jnp.zeros_like(x)), axis), axis=0)
 
 
 def local(l_panels, u_panels, panel_fill, copy_fill, sep_panels, sep_owner):

time: 1020 us -> 1390 us (1.36)
  the two profiles are of different devices: /device:TPU:8 before, /device:TPU:1 now
where the time goes in v1:
time: 1390 us
  waiting for transfers between devices  1270 us (91%)
  other arithmetic  66.6 us (5%)
  starting transfers between devices  20.4 us (1%)
  between operations  15.7 us (1%)
  matrix products  15.6 us (1%)
    all_gather x4, waiting for transfers between devices, spread(): lax.all_gather(jnp.where(mine, x, jnp.zeros_like(x)), axis)  956 us
    ppermute x4, waiting for transfers between devices, from_partner(): lax.ppermute(x, axis, [(i, i ^ 1 << apart) for i in range(lax.axis_size(a...  218 us
    all_gather x1, waiting for transfers between devices, local(): piece = lax.all_gather(u_panels, 'grid', axis=2, tiled=True)  90.8 us
    reduce_sum x4, other arithmetic, spread(): jnp.sum(lax.all_gather(jnp.where(mine, x, jnp.zeros_like(x)), axis), axis=0)  45.8 us
  transfers between devices with their start and end apart: 9, of which 9 were waited for; matrix products, arithmetic and copies ran while one was open for 0% of the time, Pallas kernels for 0%

profile of v1, /device:TPU:1, one launch (start us, length us, event | category | flops | bytes accessed | tf_op | source)
XLA Modules:
  0.0 1386.0 jit_solution(14904285957876874924)
XLA Ops:
  6.5 0.0 copy-start
  6.5 0.0 all-gather.10.cloned.1.call-start
  6.5 0.7 all-gather.10.cloned.1.call-update
  7.3 0.0 all-gather.12.cloned.1.call-start
  7.3 1.2 reshape_squeeze.3
  8.5 0.7 convert_bitcast_fusion
  9.2 0.7 convert_bitcast_fusion.1
  9.8 0.3 broadcast_multiply_fusion
  10.2 0.2 fusion.20
  10.3 90.8 %all-gather.10.cloned.1.call-done = bf16[1,2,512,2048]{3,2,1,0:T(8,128)(2,1)} async-done(((bf16[1,2,16,2048]{3,2,1,0:T(8,128)(2,1)}), bf16[1,2,512,2048]{3,2,1,0:T(8,128)(2,1)}) %all-gather.10.cloned.1.call-update) | async-done | bytes 4194320 | tf_op jit(solution)/shard_map/all_gather | solution.py:29
  101.1 2.4 fusion.2
  103.6 0.2 mul.24
  103.8 0.2 copy-done.1
  103.9 2.5 fusion.1
  106.5 6.0 collective-permute-start
  112.5 0.0 copy-done.2
  112.5 0.6 fusion.21
  113.8 2.8 collective-permute-done
  116.6 4.4 convert_select_fusion.3
  120.9 0.0 all-gather.12.cloned.1.call-update
  121.0 0.0 all-gather.14.cloned.1.call-start
  121.0 235.3 %all-gather.12.cloned.1.call-done = bf16[8192,2048]{1,0:T(8,128)(2,1)} async-done(((bf16[256,2048]{1,0:T(8,128)(2,1)}), bf16[8192,2048]{1,0:T(8,128)(2,1)}) %all-gather.12.cloned.1.call-update) | async-done | bytes 33554448 | tf_op jit(solution)/shard_map/all_gather | solution.py:15
  356.3 11.5 reduce_sum.48
  367.7 3.4 convolution_subtract_fusion.2
  371.2 3.1 collective-permute-start.1
  374.9 44.6 %collective-permute-done.1 = f32[256,2048]{1,0:T(8,128)} collective-permute-done((f32[256,2048]{1,0:T(8,128)}, f32[256,2048]{1,0:T(8,128)}, u32[]{:S(2)}, u32[]{:S(2)}) %collective-permute-start.1) | collective-permute-done | bytes 2097184 | tf_op jit(solution)/shard_map/ppermute | solution.py:10
  419.4 4.4 convert_select_fusion.2
  423.8 0.0 all-gather.14.cloned.1.call-update
  423.9 0.0 all-gather.16.cloned.1.call-start
  423.9 237.1 %all-gather.14.cloned.1.call-done = bf16[8192,2048]{1,0:T(8,128)(2,1)} async-done(((bf16[256,2048]{1,0:T(8,128)(2,1)}), bf16[8192,2048]{1,0:T(8,128)(2,1)}) %all-gather.14.cloned.1.call-update) | async-done | bytes 33554448 | tf_op jit(solution)/shard_map/all_gather | solution.py:15
  661.0 11.5 reduce_sum.49
  672.5 3.4 convolution_subtract_fusion.1
  675.8 4.0 collective-permute-start.2
  680.4 90.0 %collective-permute-done.2 = f32[256,2048]{1,0:T(8,128)} collective-permute-done((f32[256,2048]{1,0:T(8,128)}, f32[256,2048]{1,0:T(8,128)}, u32[]{:S(2)}, u32[]{:S(2)}) %collective-permute-start.2) | collective-permute-done | bytes 2097184 | tf_op jit(solution)/shard_map/ppermute | solution.py:10
  770.5 4.4 convert_select_fusion.1
  774.8 0.0 all-gather.16.cloned.1.call-update
  774.8 0.0 all-gather.18.cloned.1.call-start
  774.9 236.7 %all-gather.16.cloned.1.call-done = bf16[8192,2048]{1,0:T(8,128)(2,1)} async-done(((bf16[256,2048]{1,0:T(8,128)(2,1)}), bf16[8192,2048]{1,0:T(8,128)(2,1)}) %all-gather.16.cloned.1.call-update) | async-done | bytes 33554448 | tf_op jit(solution)/shard_map/all_gather | solution.py:15
  1011.5 11.5 reduce_sum.50
  1023.0 3.4 convolution_subtract_fusion
  1026.4 7.1 collective-permute-start.3
  1034.1 80.9 %collective-permute-done.3 = f32[256,2048]{1,0:T(8,128)} collective-permute-done((f32[256,2048]{1,0:T(8,128)}, f32[256,2048]{1,0:T(8,128)}, u32[]{:S(2)}, u32[]{:S(2)}) %collective-permute-start.3) | collective-permute-done | bytes 2097184 | tf_op jit(solution)/shard_map/ppermute | solution.py:10
  1115.0 4.4 convert_select_fusion
  1119.4 0.0 all-gather.18.cloned.1.call-update
  1119.5 246.5 %all-gather.18.cloned.1.call-done = bf16[8192,2048]{1,0:T(8,128)(2,1)} async-done(((bf16[256,2048]{1,0:T(8,128)(2,1)}), bf16[8192,2048]{1,0:T(8,128)(2,1)}) %all-gather.18.cloned.1.call-update) | async-done | bytes 33554448 | tf_op jit(solution)/shard_map/all_gather | solution.py:15
  1366.0 11.5 reduce_sum.51
  1377.5 0.4 fusion.7
  1377.9 1.6 dynamic-slice_subtract_fusion
  (3 shorter events, 0.0 us)
Async XLA Ops:
  6.5 361.2 %copy-start = (bf16[15,256,256]{2,1,0:T(8,128)(2,1)S(1)}, bf16[15,256,256]{2,1,0:T(8,128)(2,1)}, u32[]{:S(2)}) copy-start(bf16[15,256,256]{2,1,0:T(8,128)(2,1)} %param.10) | copy-start | bytes 5898244
  6.5 94.6 %all-gather.10.cloned.1.call-start = ((), (), s32[]{:S(2)}) async-start(), calls=%async_computation | async-start | bytes 4325376 | tf_op jit(solution)/shard_map/all_gather | solution.py:29
  7.3 349.0 %all-gather.12.cloned.1.call-start = ((), (), s32[]{:S(2)}) async-start(), calls=%async_computation.1 | async-start | bytes 34603008 | tf_op jit(solution)/shard_map/all_gather | solution.py:15
  101.1 2.8 copy-start.1
  103.9 8.6 copy-start.2
  106.5 10.1 collective-permute-start
  121.0 540.1 %all-gather.14.cloned.1.call-start = ((), (), s32[]{:S(2)}) async-start(), calls=%async_computation.2 | async-start | bytes 34603008 | tf_op jit(solution)/shard_map/all_gather | solution.py:15
  371.2 48.3 %collective-permute-start.1 = (f32[256,2048]{1,0:T(8,128)}, f32[256,2048]{1,0:T(8,128)}, u32[]{:S(2)}, u32[]{:S(2)}) collective-permute-start(f32[256,2048]{1,0:T(8,128)} %convolution_subtract_fusion.2), channel_id=1, source_target_pairs={{0,64},{32,96},{64,0},{96,32},{128,192},{160,224},{192,128},{224,1... | collective-permute-start | bytes 6291464 | tf_op jit(solution)/shard_map/ppermute | solution.py:10
  423.9 587.7 %all-gather.16.cloned.1.call-start = ((), (), s32[]{:S(2)}) async-start(), calls=%async_computation.3 | async-start | bytes 34603008 | tf_op jit(solution)/shard_map/all_gather | solution.py:15
  675.8 94.6 %collective-permute-start.2 = (f32[256,2048]{1,0:T(8,128)}, f32[256,2048]{1,0:T(8,128)}, u32[]{:S(2)}, u32[]{:S(2)}) collective-permute-start(f32[256,2048]{1,0:T(8,128)} %convolution_subtract_fusion.1), channel_id=1, source_target_pairs={{0,128},{32,160},{64,192},{96,224},{128,0},{160,32},{192,64},{224,... | collective-permute-start | bytes 6291464 | tf_op jit(solution)/shard_map/ppermute | solution.py:10
  774.8 591.2 %all-gather.18.cloned.1.call-start = ((), (), s32[]{:S(2)}) async-start(), calls=%async_computation.4 | async-start | bytes 34603008 | tf_op jit(solution)/shard_map/all_gather | solution.py:15
  1026.4 88.6 %collective-permute-start.3 = (f32[256,2048]{1,0:T(8,128)}, f32[256,2048]{1,0:T(8,128)}, u32[]{:S(2)}, u32[]{:S(2)}) collective-permute-start(f32[256,2048]{1,0:T(8,128)} %convolution_subtract_fusion), channel_id=1, source_target_pairs={{0,256},{32,288},{64,320},{96,352},{128,384},{160,416},{192,448},{... | collective-permute-start | bytes 6291464 | tf_op jit(solution)/shard_map/ppermute | solution.py:10
Sparse Core Ops, SparseCore 0:
  10.5 90.5 all-gather.9
  121.1 235.1 all-gather.11
  424.0 237.0 all-gather.13
  775.0 236.5 all-gather.15
  1119.6 246.3 all-gather.17
